TPU v7x, 512 devices: a whole 4x8x8 slice. The times are simulated.
512 devices in a mesh: dp: 8 (over y), expert: 64 (over x, z, core).
Axes of the slice: x: 4, y: 8, z: 8, core: 2. Of those that a mesh axis runs over, the one named last changes fastest.
Arguments:
- hidden_in: bfloat16 [16384, 2880], P('expert', 'dp'), may hold values from -70 to 70
- norm_gain: float32 [2880], P('dp'), may hold values from 0.25 to 1.75
- expert_ids: int32 [16384, 4], P('expert'), may hold values from 0 to 63, all different within a row; in each aligned block of 256 rows (0 to 255, 256 to 511, ...) at most 24 rows name the same one
- route_weights: float32 [16384, 4], P('expert'), may hold values from 0.1 to 0.5
- gate_weight: bfloat16 [64, 1440, 2880], P('expert', 'dp'), may hold values from -0.109375 to 0.109375
- up_weight: bfloat16 [64, 1440, 2880], P('expert', 'dp'), may hold values from -0.109375 to 0.109375
- down_weight: bfloat16 [64, 1440, 2880], P('expert', None, 'dp'), may hold values from -0.15625 to 0.15625
Outputs:
- expert_out: bfloat16 [16384, 2880], P('expert', 'dp')
- peaks: float32 [16384], P('expert')
Inputs may be any that keep to these rules, and one draw needn't show every extreme that they name: `expert_ids`: the 4 experts of a token differ. Among the 256 tokens of one index of expert, no expert is named more than 24 times, a bound that some block reaches.
All inputs are finite; a program needn't handle non-finite values.
Results may differ from a plain program's by a relative error of at most 0.025.
Values may be sent and summed in bfloat16 or wider, within the bound.
A program may use at most 64 MiB of HBM per device.

v0:
```python
import jax
import jax.numpy as jnp
from jax import lax
from jax.sharding import PartitionSpec as P

D = 2880
TOP = 4


def shards(hidden_in, norm_gain, expert_ids, route_weights, gate_weight, up_weight, down_weight):
    tok_count = hidden_in.shape[0]
    owners = lax.axis_size("expert")
    capacity = 6 * tok_count // owners
    widened = hidden_in.astype(jnp.float32)
    totals = lax.psum(jnp.sum(widened * widened, axis=1), "dp")
    inverse = lax.rsqrt(totals / D + 1e-05)
    normed = widened * inverse[:, None] * norm_gain
    peaks = lax.pmax(jnp.max(jnp.abs(normed), axis=1), "dp")
    token_scale = ((peaks + 1e-06) / 448.0).astype(jnp.bfloat16)
    payload = (normed / token_scale.astype(jnp.float32)[:, None]).astype(jnp.bfloat16)
    flat_ids = expert_ids.reshape(-1)
    pair_count = flat_ids.shape[0]
    one_hot = (flat_ids[:, None] == jnp.arange(owners, dtype=jnp.int32)[None, :]).astype(
        jnp.bfloat16
    )
    pair_index = jnp.arange(pair_count, dtype=jnp.int32)
    earlier_pairs = (pair_index[:, None] > pair_index[None, :]).astype(jnp.bfloat16)
    before = jnp.dot(earlier_pairs, one_hot, preferred_element_type=jnp.float32)
    slot_rank = jnp.sum(before * one_hot.astype(jnp.float32), axis=1).astype(jnp.int32)
    dest_slot = flat_ids * capacity + slot_rank
    source_row = pair_index // TOP
    slot_total = owners * capacity
    out_scale = jnp.zeros((slot_total,), jnp.bfloat16).at[dest_slot].set(token_scale[source_row])
    gate_local = gate_weight[0]
    up_local = up_weight[0]
    full_rows = lax.all_gather(payload, "dp", axis=1, tiled=True)
    outgoing = (
        jnp.zeros((slot_total, full_rows.shape[1]), jnp.bfloat16)
        .at[dest_slot]
        .set(full_rows[source_row])
    )
    incoming, in_scale = (
        lax.all_to_all(
            outgoing.reshape(owners, capacity, -1),
            "expert",
            split_axis=0,
            concat_axis=0,
            tiled=True,
        ),
        lax.all_to_all(
            out_scale.reshape(owners, capacity), "expert", split_axis=0, concat_axis=0, tiled=True
        ),
    )
    recv_rows = incoming.reshape(slot_total, -1)
    gate_sum = jnp.einsum("sf,uf->su", recv_rows, gate_local, preferred_element_type=jnp.float32)
    up_sum = jnp.einsum("sf,uf->su", recv_rows, up_local, preferred_element_type=jnp.float32)
    row_scale = in_scale.reshape(slot_total).astype(jnp.float32)[:, None]
    gate_val = row_scale * gate_sum
    up_val = row_scale * up_sum
    hidden = (gate_val * jax.nn.sigmoid(1.702 * gate_val) * (up_val + 1.0)).astype(jnp.bfloat16)
    down_local = down_weight[0]
    expert_rows = jnp.dot(
        lax.all_gather(hidden, "dp", axis=1, tiled=True),
        down_local,
        preferred_element_type=jnp.float32,
    ).astype(jnp.bfloat16)
    returned = lax.all_to_all(
        expert_rows.reshape(owners, capacity, -1), "expert", split_axis=0, concat_axis=0, tiled=True
    ).reshape(slot_total, -1)
    picked = returned[dest_slot].astype(jnp.float32).reshape(tok_count, TOP, -1)
    expert_out = jnp.sum(picked * route_weights[:, :, None], axis=1).astype(jnp.bfloat16)
    return (expert_out, peaks)


def solution(mesh):
    in_specs = (
        P("expert", "dp"),
        P("dp"),
        P("expert", None),
        P("expert", None),
        P("expert", "dp", None),
        P("expert", "dp", None),
        P("expert", None, "dp"),
    )
    out_specs = (P("expert", "dp"), P("expert"))
    return jax.shard_map(shards, mesh=mesh, in_specs=in_specs, out_specs=out_specs, check_vma=False)
```

profile of v0, /device:TPU:1, one launch (start us, length us, event | category | flops | bytes accessed | tf_op | source)
XLA Modules:
  0.0 471.1 jit_solution(432756324814091113)
XLA Ops:
  7.2 1.1 fusion.13
  8.3 14.7 %psum.7 = f32[256]{0:T(256)S(1)} all-reduce(f32[256]{0:T(256)S(1)} %fusion.13), channel_id=1, replica_groups=mesh['dp'=8,'expert'=64] {'dp'}, use_global_device_ids=true, to_apply=%region_2.0 | all-reduce | flops 256 | bytes 2048 | tf_op jit(solution)/shard_map/psum | solution.py:15
  23.0 1.1 fusion.17
  24.1 11.2 %pmax.7 = f32[256]{0:T(256)S(1)} all-reduce(f32[256]{0:T(256)S(1)} %fusion.17), channel_id=1, replica_groups=mesh['dp'=8,'expert'=64] {'dp'}, use_global_device_ids=true, to_apply=%region_4.0 | all-reduce | flops 256 | bytes 2048 | tf_op jit(solution)/shard_map/pmax | solution.py:18
  35.3 1.7 fusion.18
  37.0 0.8 copy.18
  38.9 6.5 %gather_fusion = bf16[1024]{0:T(1024)(128)(2,1)S(1)} fusion(bf16[256]{0:T(256)(128)(2,1)S(1)} %get-tuple-element.5, s32[1024]{0:T(1024)S(1)} %broadcast_clamp_fusion.1), kind=kCustom, calls=%fused_computation | custom fusion | bytes 8192 | tf_op jit(solution)/shard_map/gather | solution.py:33
  45.4 7.6 %scatter_custom_fusion = bf16[1536]{0:T(1024)(128)(2,1)S(1)} fusion(s32[1024]{0:T(1024)S(1)} %bitcast.25, bf16[1024]{0:T(1024)(128)(2,1)S(1)} %gather_fusion, bf16[]{:T(256)} %constant.12.clone.1), kind=kCustom, calls=%fused_computation.44 | custom fusion | bytes 3074 | tf_op jit(solution)/shard_map/scatter | solution.py:33
  53.7 21.5 %all-to-all-start = ((bf16[64,1,24]{2,1,0:T(2,128)(2,1)}), bf16[64,1,24]{2,1,0:T(2,128)(2,1)S(1)}, u32[]{:S(2)}, u32[]{:S(2)}) async-start(bf16[64,1,24]{2,1,0:T(2,128)(2,1)} %all_to_all.16), calls=%async_computation | async-start | bytes 65536 | tf_op jit(solution)/shard_map/all_to_all | solution.py:50
  75.3 10.0 %all-gather.4.cloned.1.call-done = bf16[256,2880]{0,1:T(8,128)(2,1)} async-done(((bf16[256,360]{0,1:T(8,128)(2,1)}), bf16[256,2880]{0,1:T(8,128)(2,1)}) %all-gather.4.cloned.1.call-update) | async-done | bytes 1474576 | tf_op jit(solution)/shard_map/all_gather | solution.py:36
  85.3 1.8 copy.20
  87.1 32.6 %scatter_custom_fusion.1 = bf16[1536,2880]{1,0:T(8,128)(2,1)} fusion(s32[1024]{0:T(1024)S(1)} %bitcast.26, bf16[256,2880]{1,0:T(8,128)(2,1)S(1)} %copy.20, s32[1024]{0:T(1024)S(1)} %broadcast_clamp_fusion.1, bf16[]{:T(256)} %constant.12.clone.1), kind=kCustom, calls=%fused_computation.5 | custom fusion | bytes 8847362 | tf_op jit(solution)/shard_map/scatter | solution.py:40
  119.7 15.4 %all-to-all-start.1 = ((bf16[64,24,2880]{2,1,0:T(8,128)(2,1)}), bf16[64,24,2880]{2,1,0:T(8,128)(2,1)}, u32[]{:S(2)}, u32[]{:S(2)}) async-start(bf16[64,24,2880]{2,1,0:T(8,128)(2,1)} %bitcast.24), calls=%async_computation.1 | async-start | bytes 18087936 | tf_op jit(solution)/shard_map/all_to_all | solution.py:43
  135.3 199.6 %all-to-all-done.1 = bf16[64,24,2880]{2,1,0:T(8,128)(2,1)} async-done(((bf16[64,24,2880]{2,1,0:T(8,128)(2,1)}), bf16[64,24,2880]{2,1,0:T(8,128)(2,1)}, u32[]{:S(2)}, u32[]{:S(2)}) %all-to-all-start.1) | async-done | bytes 8847392 | tf_op jit(solution)/shard_map/all_to_all | solution.py:43
  334.9 6.9 %convolution_multiply_fusion.1 = f32[1536,180]{0,1:T(8,128)S(1)} fusion(bf16[1536,2880]{1,0:T(8,128)(2,1)} %bitcast.4, bf16[1,180,2880]{2,1,0:T(8,128)(2,1)S(1)} %copy-done.4, f32[1536]{0:T(1024)S(1)} %reshape.118), kind=kOutput, calls=%fused_computation.12 | convolution fusion | flops 1592801280 | bytes 10996224 | tf_op jit(solution)/shard_map/sf,uf->su/dot_general | solution.py:55
  341.8 7.7 %fusion.7 = bf16[1,180,1536]{2,1,0:T(8,128)(2,1)} fusion(bf16[1536,2880]{1,0:T(8,128)(2,1)} %bitcast.4, f32[1536,180]{0,1:T(8,128)S(1)} %convolution_multiply_fusion.1, bf16[1,180,2880]{2,1,0:T(8,128)(2,1)S(1)} %copy-done.5, f32[1536]{0:T(1024)S(1)} %reshape.118), kind=kOutput, calls=%fused_computation.16 | convolution fusion | flops 1595013120 | bytes 11549184 | tf_op jit(solution)/shard_map/sf,uf->su/dot_general | solution.py:56
  349.5 54.2 %all-gather.6.cloned.1.call-done = bf16[8,180,1536]{2,1,0:T(8,128)(2,1)} async-done(((bf16[1,180,1536]{2,1,0:T(8,128)(2,1)}), bf16[8,180,1536]{2,1,0:T(8,128)(2,1)}) %all-gather.6.cloned.1.call-update) | async-done | bytes 4423696 | tf_op jit(solution)/shard_map/all_gather | solution.py:63
  403.7 5.2 %reshape.161 = bf16[1440,1536]{1,0:T(8,128)(2,1)} reshape(bf16[8,180,1536]{2,1,0:T(8,128)(2,1)} %all-gather.6.cloned.1.call-done) | data formatting | bytes 8847360
  409.0 4.2 convolution_convert_fusion
  413.1 1.4 copy.21
  414.5 11.2 %all-to-all-start.2 = ((bf16[64,24,360]{2,1,0:T(8,128)(2,1)}), bf16[64,24,360]{2,1,0:T(8,128)(2,1)S(1)}, u32[]{:S(2)}, u32[]{:S(2)}) async-start(bf16[64,24,360]{2,1,0:T(8,128)(2,1)} %bitcast.10), calls=%async_computation.2 | async-start | bytes 2359296 | tf_op jit(solution)/shard_map/all_to_all | solution.py:67
  426.5 30.5 %all-to-all-done.2 = bf16[64,24,360]{2,1,0:T(8,128)(2,1)S(1)} async-done(((bf16[64,24,360]{2,1,0:T(8,128)(2,1)}), bf16[64,24,360]{2,1,0:T(8,128)(2,1)S(1)}, u32[]{:S(2)}, u32[]{:S(2)}) %all-to-all-start.2) | async-done | bytes 1105952 | tf_op jit(solution)/shard_map/all_to_all | solution.py:67
  457.1 3.9 gather_fusion.1
  461.4 2.0 multiply_reduce_fusion
  (35 shorter events, 4.1 us)
Async XLA Ops:
  7.2 401.8 %copy-start = (bf16[1,1440,360]{2,1,0:T(8,128)(2,1)S(1)}, bf16[1,1440,360]{2,1,0:T(8,128)(2,1)}, u32[]{:S(2)}) copy-start(bf16[1,1440,360]{2,1,0:T(8,128)(2,1)} %param.13) | copy-start | bytes 3110404
  7.2 31.4 %copy-start.1 = (s32[256,4]{0,1:T(4,128)S(1)}, s32[256,4]{0,1:T(4,128)}, u32[]{:S(2)}) copy-start(s32[256,4]{0,1:T(4,128)} %param.9) | copy-start | bytes 12292
  7.2 78.1 %all-gather.4.cloned.1.call-start = ((), (), s32[]{:S(2)}) async-start(), calls=%async_computation.3 | async-start | bytes 1658880 | tf_op jit(solution)/shard_map/all_gather | solution.py:36
  35.3 10.1 %copy-start.3 = (f32[256]{0:T(256)}, f32[256]{0:T(256)S(1)}, u32[]{:S(2)}) copy-start(f32[256]{0:T(256)S(1)} %pmax.7) | copy-start | bytes 3076
  53.7 65.9 %all-to-all-start = ((bf16[64,1,24]{2,1,0:T(2,128)(2,1)}), bf16[64,1,24]{2,1,0:T(2,128)(2,1)S(1)}, u32[]{:S(2)}, u32[]{:S(2)}) async-start(bf16[64,1,24]{2,1,0:T(2,128)(2,1)} %all_to_all.16), calls=%async_computation | async-start | bytes 65536 | tf_op jit(solution)/shard_map/all_to_all | solution.py:50
  119.7 215.2 %copy-start.4 = (bf16[1,180,2880]{2,1,0:T(8,128)(2,1)S(1)}, bf16[1,180,2880]{2,1,0:T(8,128)(2,1)}, u32[]{:S(2)}) copy-start(bf16[1,180,2880]{2,1,0:T(8,128)(2,1)} %param.11) | copy-start | bytes 3110404
  119.7 215.2 %all-to-all-start.1 = ((bf16[64,24,2880]{2,1,0:T(8,128)(2,1)}), bf16[64,24,2880]{2,1,0:T(8,128)(2,1)}, u32[]{:S(2)}, u32[]{:S(2)}) async-start(bf16[64,24,2880]{2,1,0:T(8,128)(2,1)} %bitcast.24), calls=%async_computation.1 | async-start | bytes 18087936 | tf_op jit(solution)/shard_map/all_to_all | solution.py:43
  135.1 268.7 %all-gather.6.cloned.1.call-start = ((), (), s32[]{:S(2)}) async-start(), calls=%async_computation.4 | async-start | bytes 5087232 | tf_op jit(solution)/shard_map/all_gather | solution.py:63
  334.9 6.9 %copy-start.5 = (bf16[1,180,2880]{2,1,0:T(8,128)(2,1)S(1)}, bf16[1,180,2880]{2,1,0:T(8,128)(2,1)}, u32[]{:S(2)}) copy-start(bf16[1,180,2880]{2,1,0:T(8,128)(2,1)} %param.12) | copy-start | bytes 3110404
  414.5 11.2 %copy-start.2 = (f32[256,4]{0,1:T(4,128)S(1)}, f32[256,4]{0,1:T(4,128)}, u32[]{:S(2)}) copy-start(f32[256,4]{0,1:T(4,128)} %param.10) | copy-start | bytes 12292
  414.5 42.5 %all-to-all-start.2 = ((bf16[64,24,360]{2,1,0:T(8,128)(2,1)}), bf16[64,24,360]{2,1,0:T(8,128)(2,1)S(1)}, u32[]{:S(2)}, u32[]{:S(2)}) async-start(bf16[64,24,360]{2,1,0:T(8,128)(2,1)} %bitcast.10), calls=%async_computation.2 | async-start | bytes 2359296 | tf_op jit(solution)/shard_map/all_to_all | solution.py:67
Sparse Core Ops, SparseCore 0:
  37.1 48.1 all-gather.3
  349.6 54.0 all-gather.5
where the time goes:
time: 472 us; the launch traced here: 471 us
  waiting for transfers between devices  294 us (62%)
  local copies, waits for them, and re-layouts  63 us (13%)
  starting transfers between devices  48.1 us (10%)
  blocking collectives  25.9 us (5%)
  matrix products  19.3 us (4%)
  between operations  14.3 us (3%)
  other arithmetic  5.97 us (1%)
    all_to_all x1, waiting for transfers between devices, shards(): lax.all_to_all(outgoing.reshape(owners, capacity, -1), 'expert', split_ax...  200 us
    all_gather x1, waiting for transfers between devices, shards(): lax.all_gather(hidden, 'dp', axis=1, tiled=True)  54.2 us
    scatter x1, local copies, waits for them, and re-layouts, shards(): outgoing = jnp.zeros((slot_total, full_rows.shape[1]), jnp.bfloat16).at[d...  32.6 us
    all_to_all x1, waiting for transfers between devices, shards(): lax.all_to_all(expert_rows.reshape(owners, capacity, -1), 'expert', split...  30.5 us
    all_to_all x1, starting transfers between devices, shards(): lax.all_to_all(out_scale.reshape(owners, capacity), 'expert', split_axis=...  21.5 us
    all_to_all x1, starting transfers between devices, shards(): lax.all_to_all(outgoing.reshape(owners, capacity, -1), 'expert', split_ax...  15.4 us
    psum x1, blocking collectives, shards(): totals = lax.psum(jnp.sum(widened * widened, axis=1), 'dp')  14.7 us
    pmax x1, blocking collectives, shards(): peaks = lax.pmax(jnp.max(jnp.abs(normed), axis=1), 'dp')  11.2 us
  transfers between devices with their start and end apart: 5, of which 4 were waited for; matrix products, arithmetic and copies ran while one was open for 11% of the time, Pallas kernels for 0%

commit v1 on v0

v1 whole, which is shorter than its diff:
```python
import jax
import jax.numpy as jnp
from jax import lax
from jax.experimental import pallas as pl
from jax.experimental.pallas import tpu as pltpu
from jax.sharding import PartitionSpec as P

D = 2880
TOP = 4
CAP = 24
MESH = pl.DeviceIdType.MESH
F32 = jnp.float32
BF16 = jnp.bfloat16

NY = 8
NX, NZ, NC = 4, 8, 2
NE = NX * NZ * NC
PARTS = NX * NC
REL = NZ
ROWS = REL * CAP
HALF = ROWS // 2
TOK = 256
FEAT = D // NY
UNITS = 180
LANES = 384
TAIL = 64
TALL = 320
SUM_ROW = TAIL + 184
NT = (((1,), (1,)), ((), ()))


def kernel(
    hid_ref, gain_ref, ids_ref, rw_ref, gate_ref, up_ref, down_ref,
    out_ref, peaks_ref,
    xs, key_s, wsel_s, pwt_s, send_s, gx, gh, wg_s, wu_s, wd_s, ret_out, ret_in, stats_s,
    acc_g, acc_u, acc_o, acc_t,
    pre_send, pre_recv, disp_send, disp_recv, x_send_s, x_recv_s, h_send_s, h_recv_s,
    ret_send, ret_recv, st_send, st_recv,
):
    my_y = lax.axis_index("dp")
    my_e = lax.axis_index("expert")
    my_x = my_e // (NZ * NC)
    my_z = (my_e // NC) % NZ
    my_c = my_e % NC
    right = (my_y + 1) % NY
    left = (my_y + NY - 1) % NY

    barrier = pltpu.get_barrier_semaphore()

    @pl.loop(1, NE)
    def _(i):
        pl.semaphore_signal(
            barrier, inc=1, device_id=(my_y, (my_e + i) % NE), device_id_type=MESH
        )

    @pl.loop(1, NY)
    def _(i):
        pl.semaphore_signal(
            barrier, inc=1, device_id=((my_y + i) % NY, my_e), device_id_type=MESH
        )

    hid = hid_ref[...].astype(F32)
    scaled = hid * gain_ref[...]
    total = jnp.sum(hid * hid, axis=1, keepdims=True)
    high = total.astype(BF16).astype(F32)
    low = total - high
    xs[1, :, 0:FEAT] = scaled.astype(BF16)
    last = xs[1, :, 256:LANES].astype(F32)
    lane = lax.broadcasted_iota(jnp.int32, (TOK, 128), 1)
    at = FEAT - 256
    last = jnp.where(lane < at, last, 0.0)
    last = jnp.where(lane == at, high, last)
    last = jnp.where(lane == at + 1, low, last)
    xs[1, :, 256:LANES] = last.astype(BF16)
    biggest = jnp.max(jnp.abs(scaled), axis=1, keepdims=True)
    pair = jnp.where(lane == 0, total, jnp.where(lane == 1, biggest, 0.0))
    stats_s[0] = pair.T[0:8, :]

    named = jnp.zeros((TOK, 128), F32)
    weight = jnp.zeros((TOK, 128), F32)
    for j in range(TOP):
        hit = ids_ref[:, j : j + 1] == lane
        named = jnp.where(hit, 1.0, named)
        weight = jnp.where(hit, rw_ref[:, j : j + 1], weight)
    named_t = named.T[0:NE, :]
    wsel_s[...] = weight.T[0:NE, :]
    earlier = (
        lax.broadcasted_iota(jnp.int32, (TOK, TOK), 0)
        < lax.broadcasted_iota(jnp.int32, (TOK, TOK), 1)
    )
    earlier = jnp.where(earlier, 1.0, 0.0).astype(BF16)
    before = jnp.dot(named_t.astype(BF16), earlier, preferred_element_type=F32)
    key_s[...] = jnp.where(named_t > 0.5, before, -1.0)

    def place(part, j, sign):
        dx, dc = part // NC, part % NC
        x = (my_x + NX + sign * dx) % NX
        z = (my_z + NZ + sign * j) % NZ
        c = (my_c + dc) % NC
        return (x * NZ + z) * NC + c

    rank = lax.broadcasted_iota(jnp.int32, (CAP, TOK), 0).astype(F32)

    def selection(part):
        picks, weighted = [], []
        for j in range(REL):
            e = place(part, j, 1)
            hit = key_s[pl.ds(e, 1), :] == rank
            picks.append(jnp.where(hit, 1.0, 0.0))
            weighted.append(jnp.where(hit, wsel_s[pl.ds(e, 1), :], 0.0))
        weighted = jnp.concatenate(weighted, axis=0)
        pwt_s[part] = weighted.T.astype(BF16)
        return jnp.concatenate(picks, axis=0).astype(BF16)

    def rows_of(pick, which):
        got = jnp.dot(pick, xs[which], preferred_element_type=F32)
        return got.reshape(REL, CAP, LANES).astype(BF16)

    def first_dispatch(j):
        return pltpu.make_async_remote_copy(
            src_ref=send_s.at[0, 1, j],
            dst_ref=gx.at[0, 1, j],
            send_sem=disp_send.at[j],
            recv_sem=disp_recv.at[j],
            device_id=(my_y, place(0, j, 1)),
            device_id_type=MESH,
        )

    def dispatch(part, j):
        return pltpu.make_async_remote_copy(
            src_ref=send_s.at[part, pl.ds(0, 3), j],
            dst_ref=gx.at[part, pl.ds(0, 3), j],
            send_sem=disp_send.at[part * REL + j],
            recv_sem=disp_recv.at[part * REL + j],
            device_id=(my_y, place(part, j, 1)),
            device_id_type=MESH,
        )

    def slot(r):
        return (r + 1) % NY

    def ring(buffer, sends, recvs, half, part, step, way, first):
        to = right if way == 0 else left
        if step < 4:
            r_from = step - 1 if way == 0 else (NY + 1 - step) % NY
            r_to = step if way == 0 else NY - step
            src = buffer.at[part, first(r_from)]
            dst = buffer.at[part, first(r_to)]
        else:
            r_from = 3 if way == 0 else 5
            rows = pl.ds(0 if way == 0 else half, half)
            src = buffer.at[part, first(r_from), rows]
            dst = buffer.at[part, first(4), rows]
        sem = part * 8 + way * 4 + step - 1
        return pltpu.make_async_remote_copy(
            src_ref=src,
            dst_ref=dst,
            send_sem=sends.at[sem],
            recv_sem=recvs.at[sem],
            device_id=(to, my_e),
            device_id_type=MESH,
        )

    def x_copy(part, step, way):
        return ring(gx, x_send_s, x_recv_s, REL // 2, part, step, way, slot)

    def h_copy(part, step, way):
        return ring(gh, h_send_s, h_recv_s, HALF // 2, part, step, way, lambda r: r)

    def start(copy, part, step):
        for way in range(2):
            copy(part, step, way).start()

    def arrived(copy, part, step):
        for way in range(2):
            copy(part, step, way).wait_recv()

    def give_back(part, j):
        return pltpu.make_async_remote_copy(
            src_ref=ret_out.at[part, j],
            dst_ref=ret_in.at[part, j],
            send_sem=ret_send.at[part * REL + j],
            recv_sem=ret_recv.at[part * REL + j],
            device_id=(my_y, place(part, j, -1)),
            device_id_type=MESH,
        )

    def greet(to, which, sem):
        return pltpu.make_async_remote_copy(
            src_ref=xs.at[1],
            dst_ref=xs.at[which],
            send_sem=pre_send.at[sem],
            recv_sem=pre_recv.at[sem],
            device_id=(to, my_e),
            device_id_type=MESH,
        )

    def stat_copy(i):
        return pltpu.make_async_remote_copy(
            src_ref=stats_s.at[0],
            dst_ref=stats_s.at[i],
            send_sem=st_send.at[i],
            recv_sem=st_recv.at[i],
            device_id=((my_y + i) % NY, my_e),
            device_id_type=MESH,
        )

    pick = selection(0)
    send_s[0, 1] = rows_of(pick, 1)
    gx[0, 1, 0] = send_s[0, 1, 0]

    pl.semaphore_wait(barrier, NE - 1 + NY - 1)

    @pl.loop(1, REL)
    def _(j):
        first_dispatch(j).start()

    greet(right, 2, 0).start()
    greet(left, 0, 1).start()

    @pl.loop(1, NY)
    def _(i):
        stat_copy(i).start()

    @pl.loop(1, REL)
    def _(j):
        first_dispatch(j).wait_recv()

    start(x_copy, 0, 1)

    greet(right, 2, 0).wait_recv()
    greet(left, 0, 1).wait_recv()

    def send_part(part):
        picked = selection(part)
        for which in range(3):
            send_s[part, which] = rows_of(picked, which)

        @pl.loop(0, REL)
        def _(j):
            dispatch(part, j).start()

    send_part(1)
    arrived(x_copy, 0, 1)
    start(x_copy, 0, 2)

    for ref in (wg_s, wu_s, wd_s):
        ref[...] = jnp.zeros_like(ref)
    for k in range(NY):
        columns = slice(k * FEAT, (k + 1) * FEAT)
        wg_s[k, TAIL : TAIL + UNITS, 0:FEAT] = gate_ref[:, columns]
        wu_s[k, TAIL : TAIL + UNITS, 0:FEAT] = up_ref[:, columns]
        wd_s[k, TAIL : TAIL + UNITS, 0:FEAT] = down_ref[k * UNITS : (k + 1) * UNITS, :]
    row16 = lax.broadcasted_iota(jnp.int32, (16, 128), 0) + (SUM_ROW - SUM_ROW % 16)
    lane16 = lax.broadcasted_iota(jnp.int32, (16, 128), 1)
    ones = (row16 == SUM_ROW) & ((lane16 == at) | (lane16 == at + 1))
    ones = jnp.where(ones, 1.0, 0.0).astype(BF16)
    base = SUM_ROW - SUM_ROW % 16
    for k in range(NY):
        wg_s[k, base : base + 16, 256:LANES] = wg_s[k, base : base + 16, 256:LANES] + ones

    @pl.loop(2, PARTS)
    def _(part):
        send_part(part)

    acc_t[...] = jnp.zeros_like(acc_t)

    def x_dot(part, r):
        k = (my_y + NY - r) % NY
        block = gx[part, slot(r)].reshape(ROWS, LANES)
        for h in range(2):
            rows = slice(h * HALF, (h + 1) * HALF)
            cut = slice(TAIL, TALL) if h == 0 else slice(0, 256)
            for acc, w in ((acc_g, wg_s), (acc_u, wu_s)):
                add = lax.dot_general(block[rows], w[k, cut, :], NT, preferred_element_type=F32)
                if r == 0:
                    acc[rows] = add
                else:
                    acc[rows] += add

    def h_dot(part, r):
        k = (my_y + NY - r) % NY
        for h in range(2):
            rows = slice(h * HALF, (h + 1) * HALF)
            cut = slice(TAIL, TALL) if h == 0 else slice(0, 256)
            lanes = slice(0, 256) if h == 0 else slice(128, 384)
            add = jnp.dot(gh[part, r, :, lanes], wd_s[k, cut, :], preferred_element_type=F32)
            if r == 0:
                acc_o[rows] = add
            else:
                acc_o[rows] += add

    def activate(part):
        halves = []
        for h in range(2):
            rows = slice(h * HALF, (h + 1) * HALF)
            at_row = SUM_ROW - TAIL if h == 0 else SUM_ROW
            g, u = acc_g[rows], acc_u[rows]
            inverse = lax.rsqrt(g[:, at_row : at_row + 1] * (1.0 / D) + 1e-05)
            g = g * inverse
            u = u * inverse
            halves.append(g * jax.nn.sigmoid(1.702 * g) * (u + 1.0))
        a, b = halves
        gh[part, 0, :, 0:128] = a[:, 0:128].astype(BF16)
        gh[part, 0, :, 128:256] = (a[:, 128:256] + b[:, 0:128]).astype(BF16)
        gh[part, 0, :, 256:384] = b[:, 128:256].astype(BF16)

    def send_back(part):
        ret_out[part] = acc_o[...].reshape(REL, CAP, LANES).astype(BF16)

        @pl.when(part == 0)
        def _():
            ret_in[0, 0] = ret_out[0, 0]

        @pl.loop(jnp.where(part == 0, 1, 0), REL)
        def _(j):
            give_back(part, j).start()

    def combine(part):
        @pl.loop(jnp.where(part == 0, 1, 0), REL)
        def _(j):
            give_back(part, j).wait_recv()

        acc_t[...] += jnp.dot(
            pwt_s[part], ret_in[part].reshape(ROWS, LANES), preferred_element_type=F32
        )

    @pl.loop(0, PARTS + 2)
    def _(i):
        has_x = i < PARTS
        has_h = (i >= 1) & (i < PARTS + 1)

        @pl.when(has_x)
        def _():
            arrived(x_copy, i, 2)
            start(x_copy, i, 3)

        @pl.when(i + 1 < PARTS)
        def _():
            @pl.loop(0, REL)
            def _(j):
                dispatch(i + 1, j).wait_recv()

            start(x_copy, i + 1, 2)

        @pl.when(has_h)
        def _():
            arrived(h_copy, i - 1, 1)
            start(h_copy, i - 1, 2)

        @pl.when(has_x)
        def _():
            for r in (0, 1, 7):
                x_dot(i, r)

        @pl.when(i >= 2)
        def _():
            arrived(h_copy, i - 2, 4)
            h_dot(i - 2, 4)
            send_back(i - 2)

        @pl.when(has_x)
        def _():
            for r in (2, 6):
                x_dot(i, r)
            arrived(x_copy, i, 3)
            start(x_copy, i, 4)

        @pl.when(has_h)
        def _():
            arrived(h_copy, i - 1, 2)
            start(h_copy, i - 1, 3)

        @pl.when(has_x)
        def _():
            for r in (3, 5):
                x_dot(i, r)

        @pl.when(has_h)
        def _():
            for r in (0, 1, 7):
                h_dot(i - 1, r)

        @pl.when(has_x)
        def _():
            arrived(x_copy, i, 4)
            x_dot(i, 4)
            activate(i)
            start(h_copy, i, 1)

        @pl.when(has_h)
        def _():
            arrived(h_copy, i - 1, 3)
            start(h_copy, i - 1, 4)
            for r in (2, 6, 3, 5):
                h_dot(i - 1, r)

        @pl.when(i >= 3)
        def _():
            combine(i - 3)

    @pl.loop(1, NY)
    def _(i):
        stat_copy(i).wait_recv()

    sums = stats_s[0]
    most = stats_s[0]
    for i in range(1, NY):
        sums = sums + stats_s[i]
        most = jnp.maximum(most, stats_s[i])
    peaks_ref[...] = most[1:2, :] * lax.rsqrt(sums[0:1, :] * (1.0 / D) + 1e-05)

    combine(PARTS - 1)
    out_ref[...] = acc_t[:, 0:FEAT].astype(BF16)

    @pl.loop(1, REL)
    def _(j):
        first_dispatch(j).wait_send()

    @pl.loop(1, PARTS)
    def _(part):
        @pl.loop(0, REL)
        def _(j):
            dispatch(part, j).wait_send()

        for way in range(2):
            for step in (2, 3, 4):
                x_copy(part, step, way).wait_send()

    for way in range(2):
        for step in (1, 2, 3, 4):
            x_copy(0, step, way).wait_send()

    @pl.loop(0, PARTS)
    def _(part):
        for way in range(2):
            for step in (1, 2, 3, 4):
                h_copy(part, step, way).wait_send()

        @pl.loop(jnp.where(part == 0, 1, 0), REL)
        def _(j):
            give_back(part, j).wait_send()

    greet(right, 2, 0).wait_send()
    greet(left, 0, 1).wait_send()

    @pl.loop(1, NY)
    def _(i):
        stat_copy(i).wait_send()


def shards(hidden_in, norm_gain, expert_ids, route_weights, gate_weight, up_weight, down_weight):
    vmem = pl.BlockSpec(memory_space=pltpu.VMEM)
    dma = pltpu.SemaphoreType.DMA
    out, peaks = pl.pallas_call(
        kernel,
        out_shape=(
            jax.ShapeDtypeStruct((TOK, FEAT), BF16),
            jax.ShapeDtypeStruct((1, TOK), F32),
        ),
        in_specs=[vmem] * 7,
        out_specs=(vmem, vmem),
        scratch_shapes=[
            pltpu.VMEM((3, TOK, LANES), BF16),
            pltpu.VMEM((NE, TOK), F32),
            pltpu.VMEM((NE, TOK), F32),
            pltpu.VMEM((PARTS, TOK, ROWS), BF16),
            pltpu.VMEM((PARTS, 3, REL, CAP, LANES), BF16),
            pltpu.VMEM((PARTS, NY, REL, CAP, LANES), BF16),
            pltpu.VMEM((PARTS, NY, HALF, LANES), BF16),
            pltpu.VMEM((NY, TALL, LANES), BF16),
            pltpu.VMEM((NY, TALL, LANES), BF16),
            pltpu.VMEM((NY, TALL, LANES), BF16),
            pltpu.VMEM((PARTS, REL, CAP, LANES), BF16),
            pltpu.VMEM((PARTS, REL, CAP, LANES), BF16),
            pltpu.VMEM((NY, 8, TOK), F32),
            pltpu.VMEM((ROWS, 256), F32),
            pltpu.VMEM((ROWS, 256), F32),
            pltpu.VMEM((ROWS, LANES), F32),
            pltpu.VMEM((TOK, LANES), F32),
            dma((2,)),
            dma((2,)),
            dma((NE,)),
            dma((NE,)),
            dma((PARTS * 8,)),
            dma((PARTS * 8,)),
            dma((PARTS * 8,)),
            dma((PARTS * 8,)),
            dma((NE,)),
            dma((NE,)),
            dma((NY,)),
            dma((NY,)),
        ],
        compiler_params=pltpu.CompilerParams(
            collective_id=0, has_side_effects=True, vmem_limit_bytes=58 * 2**20
        ),
    )(
        hidden_in,
        norm_gain.reshape(1, FEAT),
        expert_ids,
        route_weights,
        gate_weight[0],
        up_weight[0],
        down_weight[0],
    )
    return (out, peaks.reshape(TOK))


def solution(mesh):
    in_specs = (
        P("expert", "dp"),
        P("dp"),
        P("expert", None),
        P("expert", None),
        P("expert", "dp", None),
        P("expert", "dp", None),
        P("expert", None, "dp"),
    )
    out_specs = (P("expert", "dp"), P("expert"))
    return jax.shard_map(shards, mesh=mesh, in_specs=in_specs, out_specs=out_specs, check_vma=False)
```

time: 472 us -> 194 us (0.41)
  waiting for transfers between devices: 294 us -> 0 us
  Pallas kernels: 0 us -> 184 us
  local copies, waits for them, and re-layouts: 63 us -> 8.91 us
  starting transfers between devices: 48.1 us -> 0 us
  blocking collectives: 25.9 us -> 0 us
  matrix products: 19.3 us -> 0 us
  between operations: 14.3 us -> 0.64 us
  other arithmetic: 5.97 us -> 0 us
    all_to_all x3 -> x0, waiting for transfers between devices: 230 us -> none  [the longest x1 200 us: shards(): lax.all_to_all(outgoing.reshape(owners, capacity, -1), 'expert', split_ax...]
    pallas_call x0 -> x1, Pallas kernels: none -> 184 us  [shards(): pl.pallas_call(kernel, out_shape=(jax.ShapeDtypeStruct((TOK, FEAT), BF16)...]
    all_gather x2 -> x0, waiting for transfers between devices: 64.2 us -> none  [the longest x1 54.2 us: shards(): lax.all_gather(hidden, 'dp', axis=1, tiled=True)]
    all_to_all x3 -> x0, starting transfers between devices: 48.1 us -> none  [the longest x1 21.5 us: shards(): lax.all_to_all(out_scale.reshape(owners, capacity), 'expert', split_axis=...]
    scatter x2 -> x0, local copies, waits for them, and re-layouts: 40.1 us -> none  [the longest x1 32.6 us: shards(): outgoing = jnp.zeros((slot_total, full_rows.shape[1]), jnp.bfloat16).at[d...]
    dot_general x4 -> x0, matrix products: 19.3 us -> none  [the longest x1 7.7 us: shards(): jnp.einsum('sf,uf->su', recv_rows, up_local, preferred_element_type=jnp.f...]
    psum x1 -> x0, blocking collectives: 14.7 us -> none  [shards(): totals = lax.psum(jnp.sum(widened * widened, axis=1), 'dp')]
    pmax x1 -> x0, blocking collectives: 11.2 us -> none  [shards(): peaks = lax.pmax(jnp.max(jnp.abs(normed), axis=1), 'dp')]
  transfers between devices with their start and end apart: 5 -> 0, of which waited for: 4 -> 0; matrix products, arithmetic and copies ran while one was open for 11% -> 0% of each run, Pallas kernels for 0% -> 0%
where the time goes in v1:
time: 194 us; the launch traced here: 193 us
  Pallas kernels  184 us (95%)
  local copies, waits for them, and re-layouts  8.91 us (5%)
    pallas_call x1, Pallas kernels, shards(): pl.pallas_call(kernel, out_shape=(jax.ShapeDtypeStruct((TOK, FEAT), BF16)...  184 us
    unnamed x5, local copies, waits for them, and re-layouts  7.64 us

profile of v1, /device:TPU:1, one launch (start us, length us, event | category | flops | bytes accessed | tf_op | source)
XLA Modules:
  0.0 193.4 jit_solution(11498913452230379935)
XLA Ops:
  0.6 1.3 reshape.10.gain_ref
  1.9 1.5 copy.10.ids_ref
  3.4 1.5 copy.11.rw_ref
  4.8 1.7 copy.9.hid_ref
  6.6 183.8 %shard_map.86 = (bf16[256,360]{1,0:T(8,128)(2,1)}, f32[1,256]{1,0:T(1,128)}) custom-call(bf16[256,360]{1,0:T(8,128)(2,1)} %copy.9.hid_ref, f32[1,360]{1,0:T(1,128)} %reshape.10.gain_ref, s32[256,4]{1,0:T(8,128)} %copy.10.ids_ref, f32[256,4]{1,0:T(8,128)} %copy.11.rw_ref, bf16[180,2880]{1,0:T(8,128)(2,1)} %bitcast.5, bf16[180,2880]{1,0:T(8,128)(2,1)} %bitcast.6, ...), custom_call_target="tpu_custom_call" | custom-call | tf_op jit(solution)/shard_map/pallas_call | solution.py:455
  190.4 1.7 copy.12
  192.1 1.2 copy.14

commit v2 on v1

v2 whole, which is shorter than its diff:
```python
import jax
import jax.numpy as jnp
from jax import lax
from jax.experimental import pallas as pl
from jax.experimental.pallas import tpu as pltpu
from jax.sharding import PartitionSpec as P

D = 2880
TOP = 4
CAP = 24
MESH = pl.DeviceIdType.MESH
F32 = jnp.float32
BF16 = jnp.bfloat16

NY = 8
NX, NZ, NC = 4, 8, 2
NE = NX * NZ * NC
PARTS = NX * NC
REL = NZ
ROWS = REL * CAP
HALF = ROWS // 2
TOK = 256
FEAT = D // NY
UNITS = 180
LANES = 384
TAIL = 64
TALL = 320
SUM_ROW = 184
WIDE = 256
PLAIN = 1
AHEAD = PLAIN + 2
NT = (((1,), (1,)), ((), ()))


def kernel(
    hid_ref, gain_ref, ids_ref, rw_ref, gate_ref, up_ref, down_ref,
    out_ref, peaks_ref,
    xs, key_s, wsel_s, pwt_s, send_s, gx, gh, wx_s, wd_s, ret_out, ret_in, stats_s,
    acc_x, acc_o, acc_t,
    pre_send, pre_recv, disp_send, disp_recv, x_send_s, x_recv_s, h_send_s, h_recv_s,
    ret_send, ret_recv, st_send, st_recv,
):
    my_y = lax.axis_index("dp")
    my_e = lax.axis_index("expert")
    my_x = my_e // (NZ * NC)
    my_z = (my_e // NC) % NZ
    my_c = my_e % NC
    right = (my_y + 1) % NY
    left = (my_y + NY - 1) % NY

    barrier = pltpu.get_barrier_semaphore()

    @pl.loop(1, NE)
    def _(i):
        pl.semaphore_signal(
            barrier, inc=1, device_id=(my_y, (my_e + i) % NE), device_id_type=MESH
        )

    @pl.loop(1, NY)
    def _(i):
        pl.semaphore_signal(
            barrier, inc=1, device_id=((my_y + i) % NY, my_e), device_id_type=MESH
        )

    gain = jnp.broadcast_to(gain_ref[...].reshape(1, FEAT), (128, FEAT))
    gain = jnp.concatenate([gain, jnp.zeros((128, LANES - FEAT), F32)], axis=1).T[0:FEAT, :]
    hid = hid_ref[...].astype(F32)
    scaled = hid * jnp.concatenate([gain, gain], axis=1)
    total = jnp.sum(hid * hid, axis=0, keepdims=True)
    biggest = jnp.max(jnp.abs(scaled), axis=0, keepdims=True)
    high = total.astype(BF16).astype(F32)
    row = lax.broadcasted_iota(jnp.int32, (LANES - FEAT, TOK), 0)
    extra = jnp.where(row == 0, high, jnp.where(row == 1, total - high, 0.0))
    xs[1] = jnp.concatenate([scaled, extra], axis=0).astype(BF16)
    row8 = lax.broadcasted_iota(jnp.int32, (8, TOK), 0)
    stats_s[0] = jnp.where(row8 == 0, total, jnp.where(row8 == 1, biggest, 0.0))

    expert = lax.broadcasted_iota(jnp.int32, (NE, TOK), 0)
    named = jnp.zeros((NE, TOK), F32)
    weight = jnp.zeros((NE, TOK), F32)
    for j in range(TOP):
        hit = ids_ref[j : j + 1, :] == expert
        named = jnp.where(hit, 1.0, named)
        weight = jnp.where(hit, rw_ref[j : j + 1, :], weight)
    wsel_s[...] = weight
    earlier = (
        lax.broadcasted_iota(jnp.int32, (TOK, TOK), 0)
        < lax.broadcasted_iota(jnp.int32, (TOK, TOK), 1)
    )
    earlier = jnp.where(earlier, 1.0, 0.0).astype(BF16)
    before = jnp.dot(named.astype(BF16), earlier, preferred_element_type=F32)
    key_s[...] = jnp.where(named > 0.5, before, -1.0)

    def place(part, j, sign):
        dx, dc = part // NC, part % NC
        x = (my_x + NX + sign * dx) % NX
        z = (my_z + NZ + sign * j) % NZ
        c = (my_c + dc) % NC
        return (x * NZ + z) * NC + c

    rank = lax.broadcasted_iota(jnp.int32, (CAP, TOK), 0).astype(F32)

    def selection(part):
        picks, weighted = [], []
        for j in range(REL):
            e = place(part, j, 1)
            hit = key_s[pl.ds(e, 1), :] == rank
            picks.append(jnp.where(hit, 1.0, 0.0))
            weighted.append(jnp.where(hit, wsel_s[pl.ds(e, 1), :], 0.0))
        weighted = jnp.concatenate(weighted, axis=0)
        pwt_s[part] = weighted.T.astype(BF16)
        return jnp.concatenate(picks, axis=0).astype(BF16)

    def rows_of(pick, which):
        got = lax.dot_general(pick, xs[which], NT, preferred_element_type=F32)
        return got.reshape(REL, CAP, LANES).astype(BF16)

    def first(part):
        return jnp.where(part == 0, 1, 0)

    def plain_dispatch(part, j):
        return pltpu.make_async_remote_copy(
            src_ref=send_s.at[part, 1, j],
            dst_ref=gx.at[part, 1, j],
            send_sem=disp_send.at[part * REL + j],
            recv_sem=disp_recv.at[part * REL + j],
            device_id=(my_y, place(part, j, 1)),
            device_id_type=MESH,
        )

    def dispatch(part, j):
        return pltpu.make_async_remote_copy(
            src_ref=send_s.at[part, pl.ds(0, 3), j],
            dst_ref=gx.at[part, pl.ds(0, 3), j],
            send_sem=disp_send.at[part * REL + j],
            recv_sem=disp_recv.at[part * REL + j],
            device_id=(my_y, place(part, j, 1)),
            device_id_type=MESH,
        )

    def slot(r):
        return (r + 1) % NY

    def ring(buffer, sends, recvs, half, part, step, way, where):
        to = right if way == 0 else left
        if step < 4:
            r_from = step - 1 if way == 0 else (NY + 1 - step) % NY
            r_to = step if way == 0 else NY - step
            src = buffer.at[part, where(r_from)]
            dst = buffer.at[part, where(r_to)]
        else:
            r_from = 3 if way == 0 else 5
            rows = pl.ds(0 if way == 0 else half, half)
            src = buffer.at[part, where(r_from), rows]
            dst = buffer.at[part, where(4), rows]
        sem = part * 8 + way * 4 + step - 1
        return pltpu.make_async_remote_copy(
            src_ref=src,
            dst_ref=dst,
            send_sem=sends.at[sem],
            recv_sem=recvs.at[sem],
            device_id=(to, my_e),
            device_id_type=MESH,
        )

    def x_copy(part, step, way):
        return ring(gx, x_send_s, x_recv_s, REL // 2, part, step, way, slot)

    def h_copy(part, step, way):
        return ring(gh, h_send_s, h_recv_s, HALF // 2, part, step, way, lambda r: r)

    def start(copy, part, step):
        for way in range(2):
            copy(part, step, way).start()

    def arrived(copy, part, step):
        for way in range(2):
            copy(part, step, way).wait_recv()

    def left_here(copy, part, steps):
        for way in range(2):
            for step in steps:
                copy(part, step, way).wait_send()

    def give_back(part, j):
        return pltpu.make_async_remote_copy(
            src_ref=ret_out.at[part, j],
            dst_ref=ret_in.at[part, j],
            send_sem=ret_send.at[part * REL + j],
            recv_sem=ret_recv.at[part * REL + j],
            device_id=(my_y, place(part, j, -1)),
            device_id_type=MESH,
        )

    def greet(to, which, sem):
        return pltpu.make_async_remote_copy(
            src_ref=xs.at[1],
            dst_ref=xs.at[which],
            send_sem=pre_send.at[sem],
            recv_sem=pre_recv.at[sem],
            device_id=(to, my_e),
            device_id_type=MESH,
        )

    def stat_copy(i):
        return pltpu.make_async_remote_copy(
            src_ref=stats_s.at[0],
            dst_ref=stats_s.at[i],
            send_sem=st_send.at[i],
            recv_sem=st_recv.at[i],
            device_id=((my_y + i) % NY, my_e),
            device_id_type=MESH,
        )

    send_s[0, 1] = rows_of(selection(0), 1)
    gx[0, 1, 0] = send_s[0, 1, 0]
    for part in range(1, PLAIN):
        send_s[part, 1] = rows_of(selection(part), 1)

    pl.semaphore_wait(barrier, NE - 1 + NY - 1)

    greet(right, 2, 0).start()
    greet(left, 0, 1).start()
    for part in range(PLAIN):
        @pl.loop(first(part), REL)
        def _(j):
            plain_dispatch(part, j).start()

    @pl.loop(1, NY)
    def _(i):
        stat_copy(i).start()

    wx_s[...] = jnp.zeros_like(wx_s)
    for k in range(NY):
        columns = slice(k * FEAT, (k + 1) * FEAT)
        wx_s[k, 0:UNITS, 0:FEAT] = gate_ref[:, columns]
        wx_s[k, WIDE : WIDE + UNITS, 0:FEAT] = up_ref[:, columns]

    for part in range(PLAIN):
        @pl.loop(first(part), REL)
        def _(j):
            plain_dispatch(part, j).wait_recv()

        start(x_copy, part, 1)

    greet(right, 2, 0).wait_recv()
    greet(left, 0, 1).wait_recv()

    def send_part(part):
        picked = selection(part)
        for which in range(3):
            send_s[part, which] = rows_of(picked, which)

        @pl.loop(0, REL)
        def _(j):
            dispatch(part, j).start()

    @pl.loop(PLAIN, AHEAD)
    def _(part):
        send_part(part)

    def prepare():
        base = SUM_ROW - SUM_ROW % 16
        row16 = lax.broadcasted_iota(jnp.int32, (16, 128), 0) + base
        lane16 = lax.broadcasted_iota(jnp.int32, (16, 128), 1) + 256
        ones = (row16 == SUM_ROW) & ((lane16 == FEAT) | (lane16 == FEAT + 1))
        ones = jnp.where(ones, 1.0, 0.0).astype(BF16)
        for k in range(NY):
            wx_s[k, base : base + 16, 256:LANES] = wx_s[k, base : base + 16, 256:LANES] + ones
        wd_s[...] = jnp.zeros_like(wd_s)
        for k in range(NY):
            wd_s[k, TAIL : TAIL + UNITS, 0:FEAT] = down_ref[k * UNITS : (k + 1) * UNITS, :]
        acc_t[...] = jnp.zeros_like(acc_t)

    def x_dot(part, r):
        k = (my_y + NY - r) % NY
        block = gx[part, slot(r)].reshape(ROWS, LANES)
        add = lax.dot_general(block, wx_s[k], NT, preferred_element_type=F32)
        if r == 0:
            acc_x[...] = add
        else:
            acc_x[...] += add

    def h_dot(part, r):
        k = (my_y + NY - r) % NY
        for h in range(2):
            rows = slice(h * HALF, (h + 1) * HALF)
            cut = slice(TAIL, TALL) if h == 0 else slice(0, 256)
            lanes = slice(0, 256) if h == 0 else slice(128, 384)
            add = jnp.dot(gh[part, r, :, lanes], wd_s[k, cut, :], preferred_element_type=F32)
            if r == 0:
                acc_o[rows] = add
            else:
                acc_o[rows] += add

    def activate(part):
        g, u = acc_x[:, 0:WIDE], acc_x[:, WIDE : 2 * WIDE]
        inverse = lax.rsqrt(g[:, SUM_ROW : SUM_ROW + 1] * (1.0 / D) + 1e-05)
        g = g * inverse
        u = u * inverse
        hidden = g * jax.nn.sigmoid(1.702 * g) * (u + 1.0)
        a = hidden[0:HALF]
        b = pltpu.roll(hidden[HALF:ROWS], TAIL, 1)
        gh[part, 0, :, 0:128] = a[:, 0:128].astype(BF16)
        lane = lax.broadcasted_iota(jnp.int32, (HALF, 128), 1)
        middle = jnp.where(lane < TAIL, a[:, 128:256], b[:, 0:128])
        gh[part, 0, :, 128:256] = middle.astype(BF16)
        gh[part, 0, :, 256:384] = b[:, 128:256].astype(BF16)

    def send_back(part):
        ret_out[part] = acc_o[...].reshape(REL, CAP, LANES).astype(BF16)

        @pl.when(part == 0)
        def _():
            ret_in[0, 0] = ret_out[0, 0]

        @pl.loop(first(part), REL)
        def _(j):
            give_back(part, j).start()

    def combine(part):
        @pl.loop(first(part), REL)
        def _(j):
            give_back(part, j).wait_recv()

        acc_t[...] += jnp.dot(
            pwt_s[part], ret_in[part].reshape(ROWS, LANES), preferred_element_type=F32
        )

    @pl.loop(0, PARTS + 3)
    def _(i):
        in_x = i < PARTS
        in_x4 = (i >= 1) & (i <= PARTS)
        in_h = (i >= 2) & (i <= PARTS + 1)
        in_h4 = i >= 3

        @pl.when(i < PLAIN)
        def _():
            arrived(x_copy, i, 1)

        @pl.when((i >= PLAIN) & in_x)
        def _():
            @pl.loop(0, REL)
            def _(j):
                dispatch(i, j).wait_recv()

        @pl.when(in_x)
        def _():
            start(x_copy, i, 2)

        @pl.when(in_x4)
        def _():
            arrived(x_copy, i - 1, 3)
            start(x_copy, i - 1, 4)

        @pl.when(in_h)
        def _():
            arrived(h_copy, i - 2, 1)
            start(h_copy, i - 2, 2)

        @pl.when(in_h4)
        def _():
            arrived(h_copy, i - 3, 3)
            start(h_copy, i - 3, 4)

        @pl.when(i == 0)
        def _():
            prepare()

        @pl.when(i + AHEAD < PARTS)
        def _():
            send_part(i + AHEAD)

        @pl.when(in_x4)
        def _():
            for r in (0, 1, 7, 2, 6, 3, 5):
                x_dot(i - 1, r)

        @pl.when(in_x)
        def _():
            arrived(x_copy, i, 2)
            start(x_copy, i, 3)

        @pl.when(in_x4)
        def _():
            arrived(x_copy, i - 1, 4)
            x_dot(i - 1, 4)
            activate(i - 1)
            start(h_copy, i - 1, 1)

        @pl.when(in_h)
        def _():
            arrived(h_copy, i - 2, 2)
            start(h_copy, i - 2, 3)

        @pl.when(in_h4)
        def _():
            for r in (0, 1, 7, 2, 6, 3, 5):
                h_dot(i - 3, r)
            arrived(h_copy, i - 3, 4)
            h_dot(i - 3, 4)
            send_back(i - 3)

        @pl.when(i >= 4)
        def _():
            combine(i - 4)
            left_here(h_copy, i - 4, (1, 2, 3, 4))

            @pl.loop(first(i - 4), REL)
            def _(j):
                give_back(i - 4, j).wait_send()

        @pl.when((i >= 2) & (i < PARTS + 2))
        def _():
            left_here(x_copy, i - 2, (2, 3, 4))

        @pl.when(i < PLAIN)
        def _():
            left_here(x_copy, i, (1,))

            @pl.loop(first(i), REL)
            def _(j):
                plain_dispatch(i, j).wait_send()

        @pl.when((i >= PLAIN) & in_x)
        def _():
            @pl.loop(0, REL)
            def _(j):
                dispatch(i, j).wait_send()

        @pl.when(i == 3)
        def _():
            greet(right, 2, 0).wait_send()
            greet(left, 0, 1).wait_send()

            @pl.loop(1, NY)
            def _(n):
                stat_copy(n).wait()

            sums = stats_s[0]
            most = stats_s[0]
            for n in range(1, NY):
                sums = sums + stats_s[n]
                most = jnp.maximum(most, stats_s[n])
            peaks = most[1:2, :] * lax.rsqrt(sums[0:1, :] * (1.0 / D) + 1e-05)
            peaks_ref[...] = peaks.reshape(peaks_ref.shape)

    left_here(h_copy, PARTS - 1, (1, 2, 3, 4))
    combine(PARTS - 1)
    out_ref[...] = acc_t[...].T[0:FEAT, :].astype(BF16)

    @pl.loop(0, REL)
    def _(j):
        give_back(PARTS - 1, j).wait_send()


def shards(hidden_in, norm_gain, expert_ids, route_weights, gate_weight, up_weight, down_weight):
    vmem = pl.BlockSpec(memory_space=pltpu.VMEM)
    dma = pltpu.SemaphoreType.DMA
    out, peaks = pl.pallas_call(
        kernel,
        out_shape=(
            jax.ShapeDtypeStruct((FEAT, TOK), BF16),
            jax.ShapeDtypeStruct((TOK,), F32),
        ),
        in_specs=[vmem] * 7,
        out_specs=(vmem, vmem),
        scratch_shapes=[
            pltpu.VMEM((3, LANES, TOK), BF16),
            pltpu.VMEM((NE, TOK), F32),
            pltpu.VMEM((NE, TOK), F32),
            pltpu.VMEM((PARTS, TOK, ROWS), BF16),
            pltpu.VMEM((PARTS, 3, REL, CAP, LANES), BF16),
            pltpu.VMEM((PARTS, NY, REL, CAP, LANES), BF16),
            pltpu.VMEM((PARTS, NY, HALF, LANES), BF16),
            pltpu.VMEM((NY, 2 * WIDE, LANES), BF16),
            pltpu.VMEM((NY, TALL, LANES), BF16),
            pltpu.VMEM((PARTS, REL, CAP, LANES), BF16),
            pltpu.VMEM((PARTS, REL, CAP, LANES), BF16),
            pltpu.VMEM((NY, 8, TOK), F32),
            pltpu.VMEM((ROWS, 2 * WIDE), F32),
            pltpu.VMEM((ROWS, LANES), F32),
            pltpu.VMEM((TOK, LANES), F32),
            dma((2,)),
            dma((2,)),
            dma((NE,)),
            dma((NE,)),
            dma((PARTS * 8,)),
            dma((PARTS * 8,)),
            dma((PARTS * 8,)),
            dma((PARTS * 8,)),
            dma((NE,)),
            dma((NE,)),
            dma((NY,)),
            dma((NY,)),
        ],
        compiler_params=pltpu.CompilerParams(
            collective_id=0, has_side_effects=True, vmem_limit_bytes=58 * 2**20
        ),
    )(
        hidden_in.T,
        norm_gain,
        expert_ids.T,
        route_weights.T,
        gate_weight[0],
        up_weight[0],
        down_weight[0],
    )
    return (out.T, peaks)


def solution(mesh):
    in_specs = (
        P("expert", "dp"),
        P("dp"),
        P("expert", None),
        P("expert", None),
        P("expert", "dp", None),
        P("expert", "dp", None),
        P("expert", None, "dp"),
    )
    out_specs = (P("expert", "dp"), P("expert"))
    return jax.shard_map(shards, mesh=mesh, in_specs=in_specs, out_specs=out_specs, check_vma=False)
```

time: 194 us -> 168 us (0.87)
  Pallas kernels: 184 us -> 165 us
  local copies, waits for them, and re-layouts: 8.91 us -> 2.79 us
    pallas_call x1, Pallas kernels: 184 us -> 165 us  [shards(): pl.pallas_call(kernel, out_shape=(jax.ShapeDtypeStruct((FEAT, TOK), BF16)...]
    unnamed x5 -> x2, local copies, waits for them, and re-layouts: 7.64 us -> 2.79 us
where the time goes in v2:
time: 168 us
  Pallas kernels  165 us (98%)
  local copies, waits for them, and re-layouts  2.79 us (2%)
    pallas_call x1, Pallas kernels, shards(): pl.pallas_call(kernel, out_shape=(jax.ShapeDtypeStruct((FEAT, TOK), BF16)...  165 us

profile of v2, /device:TPU:1, one launch (start us, length us, event | category | flops | bytes accessed | tf_op | source)
XLA Modules:
  0.0 168.0 jit_solution(3636583225595747498)
XLA Ops:
  0.6 164.6 %shard_map.86 = (bf16[360,256]{1,0:T(8,128)(2,1)}, f32[256]{0:T(256)}) custom-call(bf16[360,256]{1,0:T(8,128)(2,1)} %bitcast.10, f32[360]{0:T(512)} %gain_ref.1, s32[4,256]{1,0:T(4,128)} %bitcast.12, f32[4,256]{1,0:T(4,128)} %bitcast.13, bf16[180,2880]{1,0:T(8,128)(2,1)} %bitcast.8, bf16[180,2880]{1,0:T(8,128)(2,1)} %bitcast.9, bf16[1440,360]{1,0:T(8,128)(2,1)} %bitcast.7), custom_call_target="tpu_custom_call" | custom-call | tf_op jit(solution)/shard_map/pallas_call | solution.py:460
  165.2 1.6 copy.11
  166.8 1.2 copy.12

commit v3 on v2

--- a/solution.py
+++ b/solution.py
@@ -16,6 +16,8 @@
 NX, NZ, NC = 4, 8, 2
 NE = NX * NZ * NC
 PARTS = NX * NC
+LAST = PARTS - 1
+BROAD = 6
 REL = NZ
 ROWS = REL * CAP
 HALF = ROWS // 2
@@ -27,8 +29,8 @@
 TALL = 320
 SUM_ROW = 184
 WIDE = 256
-PLAIN = 1
-AHEAD = PLAIN + 2
+AHEAD = 4
+OWN = 2
 NT = (((1,), (1,)), ((), ()))
 
 
@@ -37,7 +39,7 @@
     out_ref, peaks_ref,
     xs, key_s, wsel_s, pwt_s, send_s, gx, gh, wx_s, wd_s, ret_out, ret_in, stats_s,
     acc_x, acc_o, acc_t,
-    pre_send, pre_recv, disp_send, disp_recv, x_send_s, x_recv_s, h_send_s, h_recv_s,
+    pre_send, pre_recv, disp_send, disp_recv, side_send, side_recv, x_send_s, x_recv_s, h_send_s, h_recv_s,
     ret_send, ret_recv, st_send, st_recv,
 ):
     my_y = lax.axis_index("dp")
@@ -71,7 +73,7 @@
     high = total.astype(BF16).astype(F32)
     row = lax.broadcasted_iota(jnp.int32, (LANES - FEAT, TOK), 0)
     extra = jnp.where(row == 0, high, jnp.where(row == 1, total - high, 0.0))
-    xs[1] = jnp.concatenate([scaled, extra], axis=0).astype(BF16)
+    xs[OWN] = jnp.concatenate([scaled, extra], axis=0).astype(BF16)
     row8 = lax.broadcasted_iota(jnp.int32, (8, TOK), 0)
     stats_s[0] = jnp.where(row8 == 0, total, jnp.where(row8 == 1, biggest, 0.0))
 
@@ -92,9 +94,10 @@
     key_s[...] = jnp.where(named > 0.5, before, -1.0)
 
     def place(part, j, sign):
-        dx, dc = part // NC, part % NC
+        turn = (part + 1) % PARTS
+        dx, dc, dz = turn // NC, turn % NC, j
         x = (my_x + NX + sign * dx) % NX
-        z = (my_z + NZ + sign * j) % NZ
+        z = (my_z + NZ + sign * dz) % NZ
         c = (my_c + dc) % NC
         return (x * NZ + z) * NC + c
 
@@ -116,30 +119,32 @@
         return got.reshape(REL, CAP, LANES).astype(BF16)
 
     def first(part):
-        return jnp.where(part == 0, 1, 0)
-
-    def plain_dispatch(part, j):
+        return jnp.where(part == LAST, 1, 0)
+
+    def row_copy(part, j, slots, send, recv, sem):
         return pltpu.make_async_remote_copy(
-            src_ref=send_s.at[part, 1, j],
-            dst_ref=gx.at[part, 1, j],
-            send_sem=disp_send.at[part * REL + j],
-            recv_sem=disp_recv.at[part * REL + j],
+            src_ref=send_s.at[part, slots, j],
+            dst_ref=gx.at[part, slots, j],
+            send_sem=send.at[sem],
+            recv_sem=recv.at[sem],
             device_id=(my_y, place(part, j, 1)),
             device_id_type=MESH,
         )
 
-    def dispatch(part, j):
-        return pltpu.make_async_remote_copy(
-            src_ref=send_s.at[part, pl.ds(0, 3), j],
-            dst_ref=gx.at[part, pl.ds(0, 3), j],
-            send_sem=disp_send.at[part * REL + j],
-            recv_sem=disp_recv.at[part * REL + j],
-            device_id=(my_y, place(part, j, 1)),
-            device_id_type=MESH,
-        )
+    def own_rows(part, j):
+        return row_copy(part, j, OWN, disp_send, disp_recv, part * REL + j)
+
+    def near_rows(part, j):
+        return row_copy(part, j, pl.ds(OWN - 1, 3), disp_send, disp_recv, part * REL + j)
+
+    def wide_rows(part, j):
+        return row_copy(part, j, pl.ds(0, 5), disp_send, disp_recv, part * REL + j)
+
+    def side_rows(j, way):
+        return row_copy(1, j, OWN - 1 + 2 * way, side_send, side_recv, way * REL + j)
 
     def slot(r):
-        return (r + 1) % NY
+        return (r + OWN) % NY
 
     def ring(buffer, sends, recvs, half, part, step, way, where):
         to = right if way == 0 else left
@@ -192,12 +197,13 @@
             device_id_type=MESH,
         )
 
-    def greet(to, which, sem):
+    def greet(step, way):
+        to, turn = (right, 1) if way == 0 else (left, -1)
         return pltpu.make_async_remote_copy(
-            src_ref=xs.at[1],
-            dst_ref=xs.at[which],
-            send_sem=pre_send.at[sem],
-            recv_sem=pre_recv.at[sem],
+            src_ref=xs.at[OWN + turn * (step - 1)],
+            dst_ref=xs.at[OWN + turn * step],
+            send_sem=pre_send.at[way * 2 + step - 1],
+            recv_sem=pre_recv.at[way * 2 + step - 1],
             device_id=(to, my_e),
             device_id_type=MESH,
         )
@@ -212,19 +218,20 @@
             device_id_type=MESH,
         )
 
-    send_s[0, 1] = rows_of(selection(0), 1)
-    gx[0, 1, 0] = send_s[0, 1, 0]
-    for part in range(1, PLAIN):
-        send_s[part, 1] = rows_of(selection(part), 1)
+    send_s[0, OWN] = rows_of(selection(0), OWN)
+    second = selection(1)
+    send_s[1, OWN] = rows_of(second, OWN)
 
     pl.semaphore_wait(barrier, NE - 1 + NY - 1)
 
-    greet(right, 2, 0).start()
-    greet(left, 0, 1).start()
-    for part in range(PLAIN):
-        @pl.loop(first(part), REL)
-        def _(j):
-            plain_dispatch(part, j).start()
+    greet(1, 0).start()
+    greet(1, 1).start()
+
+    @pl.loop(0, 2)
+    def _(part):
+        @pl.loop(0, REL)
+        def _(j):
+            own_rows(part, j).start()
 
     @pl.loop(1, NY)
     def _(i):
@@ -236,26 +243,52 @@
         wx_s[k, 0:UNITS, 0:FEAT] = gate_ref[:, columns]
         wx_s[k, WIDE : WIDE + UNITS, 0:FEAT] = up_ref[:, columns]
 
-    for part in range(PLAIN):
-        @pl.loop(first(part), REL)
-        def _(j):
-            plain_dispatch(part, j).wait_recv()
-
-        start(x_copy, part, 1)
-
-    greet(right, 2, 0).wait_recv()
-    greet(left, 0, 1).wait_recv()
+    @pl.loop(0, REL)
+    def _(j):
+        own_rows(0, j).wait_recv()
+
+    start(x_copy, 0, 1)
+
+    for way in range(2):
+        greet(1, way).wait_recv()
+        greet(2, way).start()
+
+    for way in range(2):
+        send_s[1, OWN - 1 + 2 * way] = rows_of(second, OWN - 1 + 2 * way)
+
+        @pl.loop(0, REL)
+        def _(j):
+            side_rows(j, way).start()
 
     def send_part(part):
         picked = selection(part)
-        for which in range(3):
+        for which in (OWN - 1, OWN, OWN + 1):
             send_s[part, which] = rows_of(picked, which)
 
         @pl.loop(0, REL)
         def _(j):
-            dispatch(part, j).start()
-
-    @pl.loop(PLAIN, AHEAD)
+            near_rows(part, j).start()
+
+    def send_wide(part):
+        @pl.when(part == BROAD)
+        def _():
+            for way in range(2):
+                greet(2, way).wait_recv()
+
+        picked = selection(part)
+        for which in range(5):
+            send_s[part, which] = rows_of(picked, which)
+
+        @pl.when(part == LAST)
+        def _():
+            for which in range(5):
+                gx[LAST, which, 0] = send_s[LAST, which, 0]
+
+        @pl.loop(first(part), REL)
+        def _(j):
+            wide_rows(part, j).start()
+
+    @pl.loop(2, AHEAD)
     def _(part):
         send_part(part)
 
@@ -310,9 +343,9 @@
     def send_back(part):
         ret_out[part] = acc_o[...].reshape(REL, CAP, LANES).astype(BF16)
 
-        @pl.when(part == 0)
-        def _():
-            ret_in[0, 0] = ret_out[0, 0]
+        @pl.when(part == LAST)
+        def _():
+            ret_in[LAST, 0] = ret_out[LAST, 0]
 
         @pl.loop(first(part), REL)
         def _(j):
@@ -327,111 +360,140 @@
             pwt_s[part], ret_in[part].reshape(ROWS, LANES), preferred_element_type=F32
         )
 
-    @pl.loop(0, PARTS + 3)
+    @pl.loop(0, PARTS + 7)
     def _(i):
-        in_x = i < PARTS
-        in_x4 = (i >= 1) & (i <= PARTS)
-        in_h = (i >= 2) & (i <= PARTS + 1)
-        in_h4 = i >= 3
-
-        @pl.when(i < PLAIN)
-        def _():
-            arrived(x_copy, i, 1)
-
-        @pl.when((i >= PLAIN) & in_x)
+        def when(part):
+            return pl.when((part >= 0) & (part < PARTS))
+
+        @when(i - 2)
+        def _():
+            arrived(x_copy, i - 2, 3)
+            start(x_copy, i - 2, 4)
+
+        @pl.when((i >= 1) & (i - 1 < BROAD))
+        def _():
+            arrived(x_copy, i - 1, 2)
+            start(x_copy, i - 1, 3)
+
+        for step in (2, 3, 4):
+            @when(i - 2 - step)
+            def _():
+                arrived(h_copy, i - 2 - step, step - 1)
+                start(h_copy, i - 2 - step, step)
+
+        @when(i - 3)
+        def _():
+            for r in (0, 1, 7, 2, 6, 3, 5):
+                x_dot(i - 3, r)
+            arrived(x_copy, i - 3, 4)
+            x_dot(i - 3, 4)
+            activate(i - 3)
+            start(h_copy, i - 3, 1)
+
+        @pl.when(i == 0)
+        def _():
+            arrived(x_copy, 0, 1)
+
+        @pl.when(i == 1)
         def _():
             @pl.loop(0, REL)
             def _(j):
-                dispatch(i, j).wait_recv()
-
-        @pl.when(in_x)
+                own_rows(1, j).wait_recv()
+                for way in range(2):
+                    side_rows(j, way).wait_recv()
+
+        @pl.when((i >= 2) & (i < BROAD))
+        def _():
+            @pl.loop(0, REL)
+            def _(j):
+                near_rows(i, j).wait_recv()
+
+        @pl.when(i < BROAD)
         def _():
             start(x_copy, i, 2)
 
-        @pl.when(in_x4)
-        def _():
-            arrived(x_copy, i - 1, 3)
-            start(x_copy, i - 1, 4)
-
-        @pl.when(in_h)
-        def _():
-            arrived(h_copy, i - 2, 1)
-            start(h_copy, i - 2, 2)
-
-        @pl.when(in_h4)
-        def _():
-            arrived(h_copy, i - 3, 3)
-            start(h_copy, i - 3, 4)
+        @pl.when((i >= BROAD) & (i < PARTS))
+        def _():
+            @pl.loop(first(i), REL)
+            def _(j):
+                wide_rows(i, j).wait_recv()
+
+            start(x_copy, i, 3)
 
         @pl.when(i == 0)
         def _():
             prepare()
 
-        @pl.when(i + AHEAD < PARTS)
+        @pl.when(i + AHEAD < BROAD)
         def _():
             send_part(i + AHEAD)
 
-        @pl.when(in_x4)
+        @pl.when((i + AHEAD >= BROAD) & (i + AHEAD < PARTS))
+        def _():
+            send_wide(i + AHEAD)
+
+        @when(i - 7)
         def _():
             for r in (0, 1, 7, 2, 6, 3, 5):
-                x_dot(i - 1, r)
-
-        @pl.when(in_x)
-        def _():
-            arrived(x_copy, i, 2)
-            start(x_copy, i, 3)
-
-        @pl.when(in_x4)
-        def _():
-            arrived(x_copy, i - 1, 4)
-            x_dot(i - 1, 4)
-            activate(i - 1)
-            start(h_copy, i - 1, 1)
-
-        @pl.when(in_h)
-        def _():
-            arrived(h_copy, i - 2, 2)
-            start(h_copy, i - 2, 3)
-
-        @pl.when(in_h4)
-        def _():
-            for r in (0, 1, 7, 2, 6, 3, 5):
-                h_dot(i - 3, r)
-            arrived(h_copy, i - 3, 4)
-            h_dot(i - 3, 4)
-            send_back(i - 3)
-
-        @pl.when(i >= 4)
-        def _():
-            combine(i - 4)
-            left_here(h_copy, i - 4, (1, 2, 3, 4))
-
-            @pl.loop(first(i - 4), REL)
-            def _(j):
-                give_back(i - 4, j).wait_send()
-
-        @pl.when((i >= 2) & (i < PARTS + 2))
-        def _():
-            left_here(x_copy, i - 2, (2, 3, 4))
-
-        @pl.when(i < PLAIN)
-        def _():
-            left_here(x_copy, i, (1,))
-
+                h_dot(i - 7, r)
+            arrived(h_copy, i - 7, 4)
+            h_dot(i - 7, 4)
+            send_back(i - 7)
+
+        @when(i - 8)
+        def _():
+            left_here(h_copy, i - 8, (1, 2, 3, 4))
+
+        @pl.when(i >= 9)
+        def _():
+            combine(i - 9)
+
+            @pl.loop(0, REL)
+            def _(j):
+                give_back(i - 9, j).wait_send()
+
+        @pl.when((i >= 4) & (i - 4 < BROAD))
+        def _():
+            left_here(x_copy, i - 4, (2,))
+
+        @when(i - 4)
+        def _():
+            left_here(x_copy, i - 4, (3, 4))
+
+        @pl.when(i == 0)
+        def _():
+            left_here(x_copy, 0, (1,))
+
+        @pl.when(i < 2)
+        def _():
+            @pl.loop(0, REL)
+            def _(j):
+                own_rows(i, j).wait_send()
+
+        @pl.when(i == 1)
+        def _():
+            @pl.loop(0, REL)
+            def _(j):
+                for way in range(2):
+                    side_rows(j, way).wait_send()
+
+        @pl.when((i >= 2) & (i < BROAD))
+        def _():
+            @pl.loop(0, REL)
+            def _(j):
+                near_rows(i, j).wait_send()
+
+        @pl.when((i >= BROAD) & (i < PARTS))
+        def _():
             @pl.loop(first(i), REL)
             def _(j):
-                plain_dispatch(i, j).wait_send()
-
-        @pl.when((i >= PLAIN) & in_x)
-        def _():
-            @pl.loop(0, REL)
-            def _(j):
-                dispatch(i, j).wait_send()
-
-        @pl.when(i == 3)
-        def _():
-            greet(right, 2, 0).wait_send()
-            greet(left, 0, 1).wait_send()
+                wide_rows(i, j).wait_send()
+
+        @pl.when(i == 4)
+        def _():
+            for way in range(2):
+                for step in (1, 2):
+                    greet(step, way).wait_send()
 
             @pl.loop(1, NY)
             def _(n):
@@ -445,13 +507,15 @@
             peaks = most[1:2, :] * lax.rsqrt(sums[0:1, :] * (1.0 / D) + 1e-05)
             peaks_ref[...] = peaks.reshape(peaks_ref.shape)
 
-    left_here(h_copy, PARTS - 1, (1, 2, 3, 4))
-    combine(PARTS - 1)
+    left_here(h_copy, LAST, (1, 2, 3, 4))
+    combine(LAST - 1)
+    combine(LAST)
     out_ref[...] = acc_t[...].T[0:FEAT, :].astype(BF16)
 
-    @pl.loop(0, REL)
-    def _(j):
-        give_back(PARTS - 1, j).wait_send()
+    for part in (LAST - 1, LAST):
+        @pl.loop(first(part), REL)
+        def _(j):
+            give_back(part, j).wait_send()
 
 
 def shards(hidden_in, norm_gain, expert_ids, route_weights, gate_weight, up_weight, down_weight):
@@ -466,11 +530,11 @@
         in_specs=[vmem] * 7,
         out_specs=(vmem, vmem),
         scratch_shapes=[
-            pltpu.VMEM((3, LANES, TOK), BF16),
+            pltpu.VMEM((5, LANES, TOK), BF16),
             pltpu.VMEM((NE, TOK), F32),
             pltpu.VMEM((NE, TOK), F32),
             pltpu.VMEM((PARTS, TOK, ROWS), BF16),
-            pltpu.VMEM((PARTS, 3, REL, CAP, LANES), BF16),
+            pltpu.VMEM((PARTS, 5, REL, CAP, LANES), BF16),
             pltpu.VMEM((PARTS, NY, REL, CAP, LANES), BF16),
             pltpu.VMEM((PARTS, NY, HALF, LANES), BF16),
             pltpu.VMEM((NY, 2 * WIDE, LANES), BF16),
@@ -481,10 +545,12 @@
             pltpu.VMEM((ROWS, 2 * WIDE), F32),
             pltpu.VMEM((ROWS, LANES), F32),
             pltpu.VMEM((TOK, LANES), F32),
-            dma((2,)),
-            dma((2,)),
+            dma((4,)),
+            dma((4,)),
             dma((NE,)),
             dma((NE,)),
+            dma((2 * REL,)),
+            dma((2 * REL,)),
             dma((PARTS * 8,)),
             dma((PARTS * 8,)),
             dma((PARTS * 8,)),

time: 168 us -> 162 us (0.964)
  Pallas kernels: 165 us -> 159 us
    pallas_call x1, Pallas kernels: 165 us -> 159 us  [shards(): pl.pallas_call(kernel, out_shape=(jax.ShapeDtypeStruct((FEAT, TOK), BF16)...]
where the time goes in v3:
time: 162 us
  Pallas kernels  159 us (98%)
  local copies, waits for them, and re-layouts  2.79 us (2%)
    pallas_call x1, Pallas kernels, shards(): pl.pallas_call(kernel, out_shape=(jax.ShapeDtypeStruct((FEAT, TOK), BF16)...  159 us

profile of v3, /device:TPU:1, one launch (start us, length us, event | category | flops | bytes accessed | tf_op | source)
XLA Modules:
  0.0 162.2 jit_solution(922090405317775213)
XLA Ops:
  0.6 158.8 %shard_map.86 = (bf16[360,256]{1,0:T(8,128)(2,1)}, f32[256]{0:T(256)}) custom-call(bf16[360,256]{1,0:T(8,128)(2,1)} %bitcast.10, f32[360]{0:T(512)} %gain_ref.1, s32[4,256]{1,0:T(4,128)} %bitcast.12, f32[4,256]{1,0:T(4,128)} %bitcast.13, bf16[180,2880]{1,0:T(8,128)(2,1)} %bitcast.8, bf16[180,2880]{1,0:T(8,128)(2,1)} %bitcast.9, bf16[1440,360]{1,0:T(8,128)(2,1)} %bitcast.7), custom_call_target="tpu_custom_call" | custom-call | tf_op jit(solution)/shard_map/pallas_call | solution.py:524
  159.4 1.6 copy.11
  161.0 1.2 copy.12

commit v4 on v3

--- a/solution.py
+++ b/solution.py
@@ -35,12 +35,12 @@
 
 
 def kernel(
-    hid_ref, gain_ref, ids_ref, rw_ref, gate_ref, up_ref, down_ref,
+    hid_ref, gain_ref, ids_ref, rw_ref, gate_hbm, up_hbm, down_hbm,
     out_ref, peaks_ref,
     xs, key_s, wsel_s, pwt_s, send_s, gx, gh, wx_s, wd_s, ret_out, ret_in, stats_s,
     acc_x, acc_o, acc_t,
     pre_send, pre_recv, disp_send, disp_recv, side_send, side_recv, x_send_s, x_recv_s, h_send_s, h_recv_s,
-    ret_send, ret_recv, st_send, st_recv,
+    ret_send, ret_recv, st_send, st_recv, gate_ref, up_ref, down_ref, load_sem,
 ):
     my_y = lax.axis_index("dp")
     my_e = lax.axis_index("expert")
@@ -63,6 +63,15 @@
         pl.semaphore_signal(
             barrier, inc=1, device_id=((my_y + i) % NY, my_e), device_id_type=MESH
         )
+
+    def loads():
+        pairs = ((gate_hbm, gate_ref), (up_hbm, up_ref), (down_hbm, down_ref))
+        return [
+            pltpu.make_async_copy(src, dst, load_sem.at[n]) for n, (src, dst) in enumerate(pairs)
+        ]
+
+    for load in loads():
+        load.start()
 
     gain = jnp.broadcast_to(gain_ref[...].reshape(1, FEAT), (128, FEAT))
     gain = jnp.concatenate([gain, jnp.zeros((128, LANES - FEAT), F32)], axis=1).T[0:FEAT, :]
@@ -238,6 +247,8 @@
         stat_copy(i).start()
 
     wx_s[...] = jnp.zeros_like(wx_s)
+    for load in loads():
+        load.wait()
     for k in range(NY):
         columns = slice(k * FEAT, (k + 1) * FEAT)
         wx_s[k, 0:UNITS, 0:FEAT] = gate_ref[:, columns]
@@ -527,7 +538,7 @@
             jax.ShapeDtypeStruct((FEAT, TOK), BF16),
             jax.ShapeDtypeStruct((TOK,), F32),
         ),
-        in_specs=[vmem] * 7,
+        in_specs=[vmem] * 4 + [pl.BlockSpec(memory_space=pl.ANY)] * 3,
         out_specs=(vmem, vmem),
         scratch_shapes=[
             pltpu.VMEM((5, LANES, TOK), BF16),
@@ -559,6 +570,10 @@
             dma((NE,)),
             dma((NY,)),
             dma((NY,)),
+            pltpu.VMEM((UNITS, D), BF16),
+            pltpu.VMEM((UNITS, D), BF16),
+            pltpu.VMEM((NY * UNITS, FEAT), BF16),
+            dma((3,)),
         ],
         compiler_params=pltpu.CompilerParams(
             collective_id=0, has_side_effects=True, vmem_limit_bytes=58 * 2**20

time: 162 us -> 161 us (level)
  no operation moved by 1% of the time
where the time goes in v4:
time: 161 us
  Pallas kernels  158 us (98%)
  local copies, waits for them, and re-layouts  2.79 us (2%)
    pallas_call x1, Pallas kernels, shards(): pl.pallas_call(kernel, out_shape=(jax.ShapeDtypeStruct((FEAT, TOK), BF16)...  158 us

profile of v4, /device:TPU:1, one launch (start us, length us, event | category | flops | bytes accessed | tf_op | source)
XLA Modules:
  0.0 161.3 jit_solution(5123162929345722232)
XLA Ops:
  0.6 157.9 %shard_map.86 = (bf16[360,256]{1,0:T(8,128)(2,1)}, f32[256]{0:T(256)}) custom-call(bf16[360,256]{1,0:T(8,128)(2,1)} %bitcast.10, f32[360]{0:T(512)} %gain_ref.1, s32[4,256]{1,0:T(4,128)} %bitcast.12, f32[4,256]{1,0:T(4,128)} %bitcast.13, bf16[180,2880]{1,0:T(8,128)(2,1)} %bitcast.8, bf16[180,2880]{1,0:T(8,128)(2,1)} %bitcast.9, bf16[1440,360]{1,0:T(8,128)(2,1)} %bitcast.7), custom_call_target="tpu_custom_call" | custom-call | tf_op jit(solution)/shard_map/pallas_call | solution.py:535
  158.5 1.6 copy.11
  160.1 1.2 copy.12
